TPU v7x, 128 devices: a whole 4x4x4 slice. The times are simulated.
128 devices in a mesh: gx: 16 (over z, y_hi, core), gy: 8 (over x, y_lo).
Axes of the slice: x: 4, y: 4 (y_hi: 2, y_lo: 2; y = y_hi * 2 + y_lo), z: 4, core: 2. Of those that a mesh axis runs over, the one named last changes fastest.
Arguments:
- state: float32 [4, 256, 128, 128], P(None, 'gx', 'gy'), may hold values from -4 to 4
- offsets: int32 [2], replicated, may hold values from 0 to 127
Outputs:
- advanced: float32 [4, 256, 128, 128], P(None, 'gx', 'gy')
All inputs are finite; a program needn't handle non-finite values.
Results may differ from a plain program's by a relative error of at most 0.00002.
Values sent between devices are 32-bit elements; how exact they have to be, the bound alone decides.
A program may use at most 64 MiB of HBM per device.

v0:
```python
import jax
import jax.numpy as jnp
from jax import lax
from jax.sharding import PartitionSpec as P

RELAX = 4
time_step = 0.2
viscosity = 0.1


def from_behind(value, axis, steps):
    count = lax.axis_size(axis)
    pairs = [(source, (source + steps) % count) for source in range(count)]
    return lax.ppermute(value, axis, pairs)


def extended(x, sides, width):
    for axis, dim in sides:
        size, length = (lax.axis_size(axis), x.shape[dim])
        up = [(i, (i + 1) % size) for i in range(size)]
        down = [(j, i) for i, j in up]
        last = lax.slice_in_dim(x, length - width, length, axis=dim)
        first = lax.slice_in_dim(x, 0, width, axis=dim)
        before = lax.ppermute(last, axis, up)
        after = lax.ppermute(first, axis, down)
        x = jnp.concatenate([before, x, after], axis=dim)
    return x


def shrink(ext):
    return ext[..., 1:-1, 1:-1, :]


def diff_x(ext):
    return (ext[..., 2:, 1:-1, :] - ext[..., :-2, 1:-1, :]) * 0.5


def diff_y(ext):
    return (ext[..., 1:-1, 2:, :] - ext[..., 1:-1, :-2, :]) * 0.5


def diff_z(center):
    return (jnp.roll(center, -1, -1) - jnp.roll(center, 1, -1)) * 0.5


def beside_all(ext):
    center = shrink(ext)
    total = ext[..., 2:, 1:-1, :] + ext[..., :-2, 1:-1, :]
    total = total + ext[..., 1:-1, 2:, :] + ext[..., 1:-1, :-2, :]
    return total + jnp.roll(center, -1, -1) + jnp.roll(center, 1, -1)


def move_rows(planes, amount):
    rows = planes.shape[2]
    span = rows * lax.axis_size("gy")
    whole = lax.all_gather(planes, "gy", axis=2, tiled=True)
    doubled = jnp.concatenate([whole, whole], axis=2)
    start = (lax.axis_index("gy") * rows + amount) % span
    return lax.dynamic_slice_in_dim(doubled, start, rows, 2)


def ghost(field, offset, width):
    lower = from_behind(field[:, -width:], "gx", 1)
    upper = from_behind(field[:, :width], "gx", -1)
    place = lax.axis_index("gx")
    count = lax.axis_size("gx")
    span = field.shape[2] * lax.axis_size("gy")
    amount = jnp.where(place == 0, -offset, offset) % span
    moved = move_rows(jnp.concatenate([lower, upper], axis=1), amount)
    left = jnp.where(place == 0, moved[:, :width], lower)
    right = jnp.where(place == count - 1, moved[:, width:], upper)
    grown = jnp.concatenate([left, field, right], axis=1)
    return extended(grown, (("gy", 2),), width)


def advance(state, offset, xpos, shear, half_width):
    mean_flow = (shear * (xpos + 0.5 - half_width))[:, None, None]
    ext = ghost(state, offset, 1)
    speed_x, speed_y, speed_z = (state[0], state[1], state[2])
    carried = speed_x * diff_x(ext) + (speed_y + mean_flow) * diff_y(ext) + speed_z * diff_z(state)
    tendency = viscosity * (beside_all(ext) - 6.0 * state) - carried
    zeros = jnp.zeros_like(speed_x)
    source = jnp.stack([zeros, -shear * speed_x, zeros, -speed_x])
    provisional = state + time_step * (tendency + source)
    velo = ghost(provisional[:3], offset, 1)
    rhs = (diff_x(velo[0]) + diff_y(velo[1]) + diff_z(provisional[2])) / time_step
    pressure = -rhs / 6.0
    for sweep in range(RELAX):
        padded = ghost(pressure[None], offset, 1)[0]
        pressure = (beside_all(padded) - rhs) / 6.0
    padded = ghost(pressure[None], offset, 1)[0]
    new_x = provisional[0] - time_step * diff_x(padded)
    new_y = provisional[1] - time_step * diff_y(padded)
    new_z = provisional[2] - time_step * diff_z(pressure)
    return jnp.stack([new_x, new_y, new_z, provisional[3]])


def local(state, offsets):
    slab = state.shape[1]
    total_x = slab * lax.axis_size("gx")
    shear = 2.0 / total_x
    half_width = total_x / 2.0
    xpos = (lax.axis_index("gx") * slab + jnp.arange(slab)).astype(jnp.float32)
    for step in range(offsets.shape[0]):
        state = advance(state, offsets[step], xpos, shear, half_width)
    return state


def solution(mesh):
    in_specs = (P(None, "gx", "gy", None), P())
    out_specs = P(None, "gx", "gy", None)
    return jax.shard_map(local, mesh=mesh, in_specs=in_specs, out_specs=out_specs, check_vma=False)
```

profile of v0, /device:TPU:14, one launch (start us, length us, event | category | flops | bytes accessed | tf_op | source)
XLA Modules:
  0.0 597.4 jit_solution(2945560103122616609)
XLA Ops:
  0.8 5.4 collective-permute-start.1
  10.6 29.0 %all_gather.42 = f32[4,2,128,128]{3,0,1,2:T(4,128)S(1)} all-gather(f32[4,2,16,128]{3,0,1,2:T(4,128)S(1)} %copy.551), channel_id=1, replica_groups=mesh['gx'=16,'gy'=8] {'gy'}, dimensions={2}, use_global_device_ids=true | all-gather | bytes 589824 | tf_op jit(solution)/shard_map/all_gather | solution.py:56
  40.0 4.2 collective-permute-start.3
  46.9 5.3 collective-permute-start.5
  53.8 28.7 %all_gather.43 = f32[3,2,128,128]{3,1,0,2:T(2,128)S(1)} all-gather(f32[3,2,16,128]{3,1,0,2:T(2,128)S(1)} %copy.558), channel_id=1, replica_groups=mesh['gx'=16,'gy'=8] {'gy'}, dimensions={2}, use_global_device_ids=true | all-gather | bytes 442368 | tf_op jit(solution)/shard_map/all_gather | solution.py:56
  88.4 4.4 collective-permute-done.7
  93.1 5.3 collective-permute-start.9
  99.8 28.2 %all_gather.44 = f32[1,2,128,128]{3,1,0,2:T(2,128)S(1)} all-gather(f32[1,2,16,128]{3,1,0,2:T(2,128)S(1)} %copy.561), channel_id=1, replica_groups=mesh['gx'=16,'gy'=8] {'gy'}, dimensions={2}, use_global_device_ids=true | all-gather | bytes 147456 | tf_op jit(solution)/shard_map/all_gather | solution.py:56
  134.5 5.3 collective-permute-start.13
  141.2 28.2 %all_gather.45 = f32[1,2,128,128]{3,1,0,2:T(2,128)S(1)} all-gather(f32[1,2,16,128]{3,1,0,2:T(2,128)S(1)} %copy.564), channel_id=1, replica_groups=mesh['gx'=16,'gy'=8] {'gy'}, dimensions={2}, use_global_device_ids=true | all-gather | bytes 147456 | tf_op jit(solution)/shard_map/all_gather | solution.py:56
  175.9 5.3 collective-permute-start.17
  182.6 28.2 %all_gather.46 = f32[1,2,128,128]{3,1,0,2:T(2,128)S(1)} all-gather(f32[1,2,16,128]{3,1,0,2:T(2,128)S(1)} %copy.567), channel_id=1, replica_groups=mesh['gx'=16,'gy'=8] {'gy'}, dimensions={2}, use_global_device_ids=true | all-gather | bytes 147456 | tf_op jit(solution)/shard_map/all_gather | solution.py:56
  217.5 5.3 collective-permute-start.21
  224.2 28.2 %all_gather.47 = f32[1,2,128,128]{3,1,0,2:T(2,128)S(1)} all-gather(f32[1,2,16,128]{3,1,0,2:T(2,128)S(1)} %copy.570), channel_id=1, replica_groups=mesh['gx'=16,'gy'=8] {'gy'}, dimensions={2}, use_global_device_ids=true | all-gather | bytes 147456 | tf_op jit(solution)/shard_map/all_gather | solution.py:56
  259.0 5.3 collective-permute-start.25
  265.7 28.2 %all_gather.48 = f32[1,2,128,128]{3,1,0,2:T(2,128)S(1)} all-gather(f32[1,2,16,128]{3,1,0,2:T(2,128)S(1)} %copy.573), channel_id=1, replica_groups=mesh['gx'=16,'gy'=8] {'gy'}, dimensions={2}, use_global_device_ids=true | all-gather | bytes 147456 | tf_op jit(solution)/shard_map/all_gather | solution.py:56
  300.4 5.3 collective-permute-start.29
  307.4 29.0 %all_gather.49 = f32[4,2,128,128]{3,0,1,2:T(4,128)S(1)} all-gather(f32[4,2,16,128]{3,0,1,2:T(4,128)S(1)} %copy.578), channel_id=1, replica_groups=mesh['gx'=16,'gy'=8] {'gy'}, dimensions={2}, use_global_device_ids=true | all-gather | bytes 589824 | tf_op jit(solution)/shard_map/all_gather | solution.py:56
  343.6 5.3 collective-permute-start.33
  350.6 28.6 %all_gather.50 = f32[3,2,128,128]{3,1,0,2:T(2,128)S(1)} all-gather(f32[3,2,16,128]{3,1,0,2:T(2,128)S(1)} %copy.585), channel_id=1, replica_groups=mesh['gx'=16,'gy'=8] {'gy'}, dimensions={2}, use_global_device_ids=true | all-gather | bytes 442368 | tf_op jit(solution)/shard_map/all_gather | solution.py:56
  379.4 4.2 collective-permute-start.34
  385.1 4.4 collective-permute-done.35
  389.9 5.3 collective-permute-start.37
  396.6 28.2 %all_gather.51 = f32[1,2,128,128]{3,1,0,2:T(2,128)S(1)} all-gather(f32[1,2,16,128]{3,1,0,2:T(2,128)S(1)} %copy.588), channel_id=1, replica_groups=mesh['gx'=16,'gy'=8] {'gy'}, dimensions={2}, use_global_device_ids=true | all-gather | bytes 147456 | tf_op jit(solution)/shard_map/all_gather | solution.py:56
  431.3 5.3 collective-permute-start.41
  438.0 28.2 %all_gather.52 = f32[1,2,128,128]{3,1,0,2:T(2,128)S(1)} all-gather(f32[1,2,16,128]{3,1,0,2:T(2,128)S(1)} %copy.591), channel_id=1, replica_groups=mesh['gx'=16,'gy'=8] {'gy'}, dimensions={2}, use_global_device_ids=true | all-gather | bytes 147456 | tf_op jit(solution)/shard_map/all_gather | solution.py:56
  472.7 5.3 collective-permute-start.45
  479.4 28.2 %all_gather.53 = f32[1,2,128,128]{3,1,0,2:T(2,128)S(1)} all-gather(f32[1,2,16,128]{3,1,0,2:T(2,128)S(1)} %copy.594), channel_id=1, replica_groups=mesh['gx'=16,'gy'=8] {'gy'}, dimensions={2}, use_global_device_ids=true | all-gather | bytes 147456 | tf_op jit(solution)/shard_map/all_gather | solution.py:56
  514.1 5.3 collective-permute-start.49
  520.8 28.2 %all_gather.54 = f32[1,2,128,128]{3,1,0,2:T(2,128)S(1)} all-gather(f32[1,2,16,128]{3,1,0,2:T(2,128)S(1)} %copy.597), channel_id=1, replica_groups=mesh['gx'=16,'gy'=8] {'gy'}, dimensions={2}, use_global_device_ids=true | all-gather | bytes 147456 | tf_op jit(solution)/shard_map/all_gather | solution.py:56
  555.6 5.3 collective-permute-start.53
  562.3 28.2 %all_gather.55 = f32[1,2,128,128]{3,1,0,2:T(2,128)S(1)} all-gather(f32[1,2,16,128]{3,1,0,2:T(2,128)S(1)} %copy.600), channel_id=1, replica_groups=mesh['gx'=16,'gy'=8] {'gy'}, dimensions={2}, use_global_device_ids=true | all-gather | bytes 147456 | tf_op jit(solution)/shard_map/all_gather | solution.py:56
  (271 shorter events, 104.4 us)
Async XLA Ops:
  0.8 9.8 %collective-permute-start = (f32[4,1,16,128]{3,2,1,0:T(8,128)S(1)}, f32[4,1,16,128]{3,2,1,0:T(8,128)S(1)}, u32[]{:S(2)}, u32[]{:S(2)}) collective-permute-start(f32[4,1,16,128]{3,2,1,0:T(8,128)S(1)} %get-tuple-element.39), channel_id=1, source_target_pairs={{0,8},{8,16},{16,24},{24,32},{32,40},{40,48},{48,56},{56,64},{64,7... | collective-permute-start | bytes 98312 | tf_op jit(solution)/shard_map/ppermute | solution.py:14
  0.8 9.8 %collective-permute-start.1 = (f32[4,1,16,128]{3,2,1,0:T(8,128)S(1)}, f32[4,1,16,128]{3,2,1,0:T(8,128)S(1)}, u32[]{:S(2)}, u32[]{:S(2)}) collective-permute-start(f32[4,1,16,128]{3,2,1,0:T(8,128)S(1)} %get-tuple-element.40), channel_id=1, source_target_pairs={{0,120},{8,0},{16,8},{24,16},{32,24},{40,32},{48,40},{56,48},{64,5... | collective-permute-start | bytes 98312 | tf_op jit(solution)/shard_map/ppermute | solution.py:14
  39.9 6.1 %collective-permute-start.2 = (f32[4,18,1,128]{3,0,2,1:T(4,128)S(1)}, f32[4,18,1,128]{3,0,2,1:T(4,128)S(1)}, u32[]{:S(2)}, u32[]{:S(2)}) collective-permute-start(f32[4,18,1,128]{3,0,2,1:T(4,128)S(1)} %copy.554), channel_id=1, source_target_pairs={{1,0},{2,1},{3,2},{4,3},{5,4},{6,5},{7,6},{0,7},{9,8},{10,9},{11,1... | collective-permute-start | bytes 110600 | tf_op jit(solution)/shard_map/ppermute | solution.py:25
  40.0 6.1 %collective-permute-start.3 = (f32[4,18,1,128]{3,0,2,1:T(4,128)S(1)}, f32[4,18,1,128]{3,0,2,1:T(4,128)S(1)}, u32[]{:S(2)}, u32[]{:S(2)}) collective-permute-start(f32[4,18,1,128]{3,0,2,1:T(4,128)S(1)} %copy.556), channel_id=1, source_target_pairs={{0,1},{1,2},{2,3},{3,4},{4,5},{5,6},{6,7},{7,0},{8,9},{9,10},{10,1... | collective-permute-start | bytes 110600 | tf_op jit(solution)/shard_map/ppermute | solution.py:24
  46.8 6.9 %collective-permute-start.4 = (f32[3,1,16,128]{3,2,1,0:T(8,128)S(1)}, f32[3,1,16,128]{3,2,1,0:T(8,128)S(1)}, u32[]{:S(2)}, u32[]{:S(2)}) collective-permute-start(f32[3,1,16,128]{3,2,1,0:T(8,128)S(1)} %get-tuple-element.32), channel_id=1, source_target_pairs={{0,8},{8,16},{16,24},{24,32},{32,40},{40,48},{48,56},{56,64},{64,7... | collective-permute-start | bytes 73736 | tf_op jit(solution)/shard_map/ppermute | solution.py:14
  46.9 6.9 %collective-permute-start.5 = (f32[3,1,16,128]{3,2,1,0:T(8,128)S(1)}, f32[3,1,16,128]{3,2,1,0:T(8,128)S(1)}, u32[]{:S(2)}, u32[]{:S(2)}) collective-permute-start(f32[3,1,16,128]{3,2,1,0:T(8,128)S(1)} %get-tuple-element.33), channel_id=1, source_target_pairs={{0,120},{8,0},{16,8},{24,16},{32,24},{40,32},{48,40},{56,48},{64,5... | collective-permute-start | bytes 73736 | tf_op jit(solution)/shard_map/ppermute | solution.py:14
  93.0 6.8 %collective-permute-start.8 = (f32[1,1,16,128]{3,2,1,0:T(8,128)S(1)}, f32[1,1,16,128]{3,2,1,0:T(8,128)S(1)}, u32[]{:S(2)}, u32[]{:S(2)}) collective-permute-start(f32[1,1,16,128]{3,2,1,0:T(8,128)S(1)} %get-tuple-element.137), channel_id=1, source_target_pairs={{0,8},{8,16},{16,24},{24,32},{32,40},{40,48},{48,56},{56,64},{64,7... | collective-permute-start | bytes 24584 | tf_op jit(solution)/shard_map/ppermute | solution.py:14
  93.1 6.7 %collective-permute-start.9 = (f32[1,1,16,128]{3,2,1,0:T(8,128)S(1)}, f32[1,1,16,128]{3,2,1,0:T(8,128)S(1)}, u32[]{:S(2)}, u32[]{:S(2)}) collective-permute-start(f32[1,1,16,128]{3,2,1,0:T(8,128)S(1)} %get-tuple-element.138), channel_id=1, source_target_pairs={{0,120},{8,0},{16,8},{24,16},{32,24},{40,32},{48,40},{56,48},{64,5... | collective-permute-start | bytes 24584 | tf_op jit(solution)/shard_map/ppermute | solution.py:14
  134.4 6.8 %collective-permute-start.12 = (f32[1,1,16,128]{3,2,1,0:T(8,128)S(1)}, f32[1,1,16,128]{3,2,1,0:T(8,128)S(1)}, u32[]{:S(2)}, u32[]{:S(2)}) collective-permute-start(f32[1,1,16,128]{3,2,1,0:T(8,128)S(1)} %get-tuple-element.135), channel_id=1, source_target_pairs={{0,8},{8,16},{16,24},{24,32},{32,40},{40,48},{48,56},{56,64},{64,7... | collective-permute-start | bytes 24584 | tf_op jit(solution)/shard_map/ppermute | solution.py:14
  134.5 6.7 %collective-permute-start.13 = (f32[1,1,16,128]{3,2,1,0:T(8,128)S(1)}, f32[1,1,16,128]{3,2,1,0:T(8,128)S(1)}, u32[]{:S(2)}, u32[]{:S(2)}) collective-permute-start(f32[1,1,16,128]{3,2,1,0:T(8,128)S(1)} %get-tuple-element.136), channel_id=1, source_target_pairs={{0,120},{8,0},{16,8},{24,16},{32,24},{40,32},{48,40},{56,48},{64,5... | collective-permute-start | bytes 24584 | tf_op jit(solution)/shard_map/ppermute | solution.py:14
  175.8 6.8 %collective-permute-start.16 = (f32[1,1,16,128]{3,2,1,0:T(8,128)S(1)}, f32[1,1,16,128]{3,2,1,0:T(8,128)S(1)}, u32[]{:S(2)}, u32[]{:S(2)}) collective-permute-start(f32[1,1,16,128]{3,2,1,0:T(8,128)S(1)} %get-tuple-element.133), channel_id=1, source_target_pairs={{0,8},{8,16},{16,24},{24,32},{32,40},{40,48},{48,56},{56,64},{64,7... | collective-permute-start | bytes 24584 | tf_op jit(solution)/shard_map/ppermute | solution.py:14
  175.9 6.7 %collective-permute-start.17 = (f32[1,1,16,128]{3,2,1,0:T(8,128)S(1)}, f32[1,1,16,128]{3,2,1,0:T(8,128)S(1)}, u32[]{:S(2)}, u32[]{:S(2)}) collective-permute-start(f32[1,1,16,128]{3,2,1,0:T(8,128)S(1)} %get-tuple-element.134), channel_id=1, source_target_pairs={{0,120},{8,0},{16,8},{24,16},{32,24},{40,32},{48,40},{56,48},{64,5... | collective-permute-start | bytes 24584 | tf_op jit(solution)/shard_map/ppermute | solution.py:14
  217.2 6.9 %collective-permute-start.20 = (f32[1,1,16,128]{3,2,1,0:T(8,128)S(1)}, f32[1,1,16,128]{3,2,1,0:T(8,128)S(1)}, u32[]{:S(2)}, u32[]{:S(2)}) collective-permute-start(f32[1,1,16,128]{3,2,1,0:T(8,128)S(1)} %get-tuple-element.131), channel_id=1, source_target_pairs={{0,8},{8,16},{16,24},{24,32},{32,40},{40,48},{48,56},{56,64},{64,7... | collective-permute-start | bytes 24584 | tf_op jit(solution)/shard_map/ppermute | solution.py:14
  217.5 6.7 %collective-permute-start.21 = (f32[1,1,16,128]{3,2,1,0:T(8,128)S(1)}, f32[1,1,16,128]{3,2,1,0:T(8,128)S(1)}, u32[]{:S(2)}, u32[]{:S(2)}) collective-permute-start(f32[1,1,16,128]{3,2,1,0:T(8,128)S(1)} %get-tuple-element.132), channel_id=1, source_target_pairs={{0,120},{8,0},{16,8},{24,16},{32,24},{40,32},{48,40},{56,48},{64,5... | collective-permute-start | bytes 24584 | tf_op jit(solution)/shard_map/ppermute | solution.py:14
  258.9 6.8 %collective-permute-start.24 = (f32[1,1,16,128]{3,2,1,0:T(8,128)S(1)}, f32[1,1,16,128]{3,2,1,0:T(8,128)S(1)}, u32[]{:S(2)}, u32[]{:S(2)}) collective-permute-start(f32[1,1,16,128]{3,2,1,0:T(8,128)S(1)} %get-tuple-element.129), channel_id=1, source_target_pairs={{0,8},{8,16},{16,24},{24,32},{32,40},{40,48},{48,56},{56,64},{64,7... | collective-permute-start | bytes 24584 | tf_op jit(solution)/shard_map/ppermute | solution.py:14
  259.0 6.7 %collective-permute-start.25 = (f32[1,1,16,128]{3,2,1,0:T(8,128)S(1)}, f32[1,1,16,128]{3,2,1,0:T(8,128)S(1)}, u32[]{:S(2)}, u32[]{:S(2)}) collective-permute-start(f32[1,1,16,128]{3,2,1,0:T(8,128)S(1)} %get-tuple-element.130), channel_id=1, source_target_pairs={{0,120},{8,0},{16,8},{24,16},{32,24},{40,32},{48,40},{56,48},{64,5... | collective-permute-start | bytes 24584 | tf_op jit(solution)/shard_map/ppermute | solution.py:14
  300.3 7.0 %collective-permute-start.28 = (f32[4,1,16,128]{3,2,1,0:T(8,128)S(1)}, f32[4,1,16,128]{3,2,1,0:T(8,128)S(1)}, u32[]{:S(2)}, u32[]{:S(2)}) collective-permute-start(f32[4,1,16,128]{3,2,1,0:T(8,128)S(1)} %get-tuple-element.25), channel_id=1, source_target_pairs={{0,8},{8,16},{16,24},{24,32},{32,40},{40,48},{48,56},{56,64},{64,7... | collective-permute-start | bytes 98312 | tf_op jit(solution)/shard_map/ppermute | solution.py:14
  300.4 6.9 %collective-permute-start.29 = (f32[4,1,16,128]{3,2,1,0:T(8,128)S(1)}, f32[4,1,16,128]{3,2,1,0:T(8,128)S(1)}, u32[]{:S(2)}, u32[]{:S(2)}) collective-permute-start(f32[4,1,16,128]{3,2,1,0:T(8,128)S(1)} %get-tuple-element.26), channel_id=1, source_target_pairs={{0,120},{8,0},{16,8},{24,16},{32,24},{40,32},{48,40},{56,48},{64,5... | collective-permute-start | bytes 98312 | tf_op jit(solution)/shard_map/ppermute | solution.py:14
  336.7 6.1 %collective-permute-start.30 = (f32[4,18,1,128]{3,0,2,1:T(4,128)S(1)}, f32[4,18,1,128]{3,0,2,1:T(4,128)S(1)}, u32[]{:S(2)}, u32[]{:S(2)}) collective-permute-start(f32[4,18,1,128]{3,0,2,1:T(4,128)S(1)} %copy.581), channel_id=1, source_target_pairs={{1,0},{2,1},{3,2},{4,3},{5,4},{6,5},{7,6},{0,7},{9,8},{10,9},{11,1... | collective-permute-start | bytes 110600 | tf_op jit(solution)/shard_map/ppermute | solution.py:25
  336.8 6.1 %collective-permute-start.31 = (f32[4,18,1,128]{3,0,2,1:T(4,128)S(1)}, f32[4,18,1,128]{3,0,2,1:T(4,128)S(1)}, u32[]{:S(2)}, u32[]{:S(2)}) collective-permute-start(f32[4,18,1,128]{3,0,2,1:T(4,128)S(1)} %copy.583), channel_id=1, source_target_pairs={{0,1},{1,2},{2,3},{3,4},{4,5},{5,6},{6,7},{7,0},{8,9},{9,10},{10,1... | collective-permute-start | bytes 110600 | tf_op jit(solution)/shard_map/ppermute | solution.py:24
  343.6 6.9 %collective-permute-start.32 = (f32[3,1,16,128]{3,2,1,0:T(8,128)S(1)}, f32[3,1,16,128]{3,2,1,0:T(8,128)S(1)}, u32[]{:S(2)}, u32[]{:S(2)}) collective-permute-start(f32[3,1,16,128]{3,2,1,0:T(8,128)S(1)} %get-tuple-element.23), channel_id=1, source_target_pairs={{0,8},{8,16},{16,24},{24,32},{32,40},{40,48},{48,56},{56,64},{64,7... | collective-permute-start | bytes 73736 | tf_op jit(solution)/shard_map/ppermute | solution.py:14
  343.6 6.9 %collective-permute-start.33 = (f32[3,1,16,128]{3,2,1,0:T(8,128)S(1)}, f32[3,1,16,128]{3,2,1,0:T(8,128)S(1)}, u32[]{:S(2)}, u32[]{:S(2)}) collective-permute-start(f32[3,1,16,128]{3,2,1,0:T(8,128)S(1)} %get-tuple-element.24), channel_id=1, source_target_pairs={{0,120},{8,0},{16,8},{24,16},{32,24},{40,32},{48,40},{56,48},{64,5... | collective-permute-start | bytes 73736 | tf_op jit(solution)/shard_map/ppermute | solution.py:14
  389.8 6.8 %collective-permute-start.36 = (f32[1,1,16,128]{3,2,1,0:T(8,128)S(1)}, f32[1,1,16,128]{3,2,1,0:T(8,128)S(1)}, u32[]{:S(2)}, u32[]{:S(2)}) collective-permute-start(f32[1,1,16,128]{3,2,1,0:T(8,128)S(1)} %get-tuple-element.117), channel_id=1, source_target_pairs={{0,8},{8,16},{16,24},{24,32},{32,40},{40,48},{48,56},{56,64},{64,7... | collective-permute-start | bytes 24584 | tf_op jit(solution)/shard_map/ppermute | solution.py:14
  389.9 6.7 %collective-permute-start.37 = (f32[1,1,16,128]{3,2,1,0:T(8,128)S(1)}, f32[1,1,16,128]{3,2,1,0:T(8,128)S(1)}, u32[]{:S(2)}, u32[]{:S(2)}) collective-permute-start(f32[1,1,16,128]{3,2,1,0:T(8,128)S(1)} %get-tuple-element.118), channel_id=1, source_target_pairs={{0,120},{8,0},{16,8},{24,16},{32,24},{40,32},{48,40},{56,48},{64,5... | collective-permute-start | bytes 24584 | tf_op jit(solution)/shard_map/ppermute | solution.py:14
  431.2 6.8 %collective-permute-start.40 = (f32[1,1,16,128]{3,2,1,0:T(8,128)S(1)}, f32[1,1,16,128]{3,2,1,0:T(8,128)S(1)}, u32[]{:S(2)}, u32[]{:S(2)}) collective-permute-start(f32[1,1,16,128]{3,2,1,0:T(8,128)S(1)} %get-tuple-element.115), channel_id=1, source_target_pairs={{0,8},{8,16},{16,24},{24,32},{32,40},{40,48},{48,56},{56,64},{64,7... | collective-permute-start | bytes 24584 | tf_op jit(solution)/shard_map/ppermute | solution.py:14
  431.3 6.7 %collective-permute-start.41 = (f32[1,1,16,128]{3,2,1,0:T(8,128)S(1)}, f32[1,1,16,128]{3,2,1,0:T(8,128)S(1)}, u32[]{:S(2)}, u32[]{:S(2)}) collective-permute-start(f32[1,1,16,128]{3,2,1,0:T(8,128)S(1)} %get-tuple-element.116), channel_id=1, source_target_pairs={{0,120},{8,0},{16,8},{24,16},{32,24},{40,32},{48,40},{56,48},{64,5... | collective-permute-start | bytes 24584 | tf_op jit(solution)/shard_map/ppermute | solution.py:14
  472.6 6.8 %collective-permute-start.44 = (f32[1,1,16,128]{3,2,1,0:T(8,128)S(1)}, f32[1,1,16,128]{3,2,1,0:T(8,128)S(1)}, u32[]{:S(2)}, u32[]{:S(2)}) collective-permute-start(f32[1,1,16,128]{3,2,1,0:T(8,128)S(1)} %get-tuple-element.113), channel_id=1, source_target_pairs={{0,8},{8,16},{16,24},{24,32},{32,40},{40,48},{48,56},{56,64},{64,7... | collective-permute-start | bytes 24584 | tf_op jit(solution)/shard_map/ppermute | solution.py:14
  472.7 6.7 %collective-permute-start.45 = (f32[1,1,16,128]{3,2,1,0:T(8,128)S(1)}, f32[1,1,16,128]{3,2,1,0:T(8,128)S(1)}, u32[]{:S(2)}, u32[]{:S(2)}) collective-permute-start(f32[1,1,16,128]{3,2,1,0:T(8,128)S(1)} %get-tuple-element.114), channel_id=1, source_target_pairs={{0,120},{8,0},{16,8},{24,16},{32,24},{40,32},{48,40},{56,48},{64,5... | collective-permute-start | bytes 24584 | tf_op jit(solution)/shard_map/ppermute | solution.py:14
  514.0 6.8 %collective-permute-start.48 = (f32[1,1,16,128]{3,2,1,0:T(8,128)S(1)}, f32[1,1,16,128]{3,2,1,0:T(8,128)S(1)}, u32[]{:S(2)}, u32[]{:S(2)}) collective-permute-start(f32[1,1,16,128]{3,2,1,0:T(8,128)S(1)} %get-tuple-element.111), channel_id=1, source_target_pairs={{0,8},{8,16},{16,24},{24,32},{32,40},{40,48},{48,56},{56,64},{64,7... | collective-permute-start | bytes 24584 | tf_op jit(solution)/shard_map/ppermute | solution.py:14
  514.1 6.7 %collective-permute-start.49 = (f32[1,1,16,128]{3,2,1,0:T(8,128)S(1)}, f32[1,1,16,128]{3,2,1,0:T(8,128)S(1)}, u32[]{:S(2)}, u32[]{:S(2)}) collective-permute-start(f32[1,1,16,128]{3,2,1,0:T(8,128)S(1)} %get-tuple-element.112), channel_id=1, source_target_pairs={{0,120},{8,0},{16,8},{24,16},{32,24},{40,32},{48,40},{56,48},{64,5... | collective-permute-start | bytes 24584 | tf_op jit(solution)/shard_map/ppermute | solution.py:14
  555.5 6.8 %collective-permute-start.52 = (f32[1,1,16,128]{3,2,1,0:T(8,128)S(1)}, f32[1,1,16,128]{3,2,1,0:T(8,128)S(1)}, u32[]{:S(2)}, u32[]{:S(2)}) collective-permute-start(f32[1,1,16,128]{3,2,1,0:T(8,128)S(1)} %get-tuple-element.105), channel_id=1, source_target_pairs={{0,8},{8,16},{16,24},{24,32},{32,40},{40,48},{48,56},{56,64},{64,7... | collective-permute-start | bytes 24584 | tf_op jit(solution)/shard_map/ppermute | solution.py:14
  555.6 6.7 %collective-permute-start.53 = (f32[1,1,16,128]{3,2,1,0:T(8,128)S(1)}, f32[1,1,16,128]{3,2,1,0:T(8,128)S(1)}, u32[]{:S(2)}, u32[]{:S(2)}) collective-permute-start(f32[1,1,16,128]{3,2,1,0:T(8,128)S(1)} %get-tuple-element.106), channel_id=1, source_target_pairs={{0,120},{8,0},{16,8},{24,16},{32,24},{40,32},{48,40},{56,48},{64,5... | collective-permute-start | bytes 24584 | tf_op jit(solution)/shard_map/ppermute | solution.py:14
  (26 other events, 121.2 us)
where the time goes:
time: 598 us; the launch traced here: 597 us
  blocking collectives  397 us (66%)
  starting transfers between devices  114 us (19%)
  waiting for transfers between devices  69.7 us (12%)
  local copies, waits for them, and re-layouts  7.44 us (1%)
    all_gather x14, blocking collectives, move_rows(): whole = lax.all_gather(planes, 'gy', axis=2, tiled=True)  397 us
    ppermute x28, starting transfers between devices, from_behind(): return lax.ppermute(value, axis, pairs)  76 us
    ppermute x14, waiting for transfers between devices, extended(): after = lax.ppermute(first, axis, down)  34.4 us
    ppermute x14, starting transfers between devices, extended(): after = lax.ppermute(first, axis, down)  20.2 us
    ppermute x28, waiting for transfers between devices, from_behind(): return lax.ppermute(value, axis, pairs)  17.7 us
    ppermute x14, starting transfers between devices, extended(): before = lax.ppermute(last, axis, up)  17.7 us
    ppermute x14, waiting for transfers between devices, extended(): before = lax.ppermute(last, axis, up)  17.6 us
  transfers between devices with their start and end apart: 56, of which 40 were waited for; matrix products, arithmetic and copies ran while one was open for 1% of the time, Pallas kernels for 0%

commit v1 on v0

--- a/solution.py
+++ b/solution.py
@@ -53,7 +53,9 @@
 def move_rows(planes, amount):
     rows = planes.shape[2]
     span = rows * lax.axis_size("gy")
-    whole = lax.all_gather(planes, "gy", axis=2, tiled=True)
+    whole = jnp.concatenate(
+        lax.all_to_all(jnp.stack([planes] * lax.axis_size("gy")), "gy", 0, 0), axis=2
+    )
     doubled = jnp.concatenate([whole, whole], axis=2)
     start = (lax.axis_index("gy") * rows + amount) % span
     return lax.dynamic_slice_in_dim(doubled, start, rows, 2)

time: 598 us -> 368 us (0.62)
  blocking collectives: 397 us -> 72.9 us
  waiting for transfers between devices: 69.7 us -> 120 us
  starting transfers between devices: 114 us -> 152 us
    all_gather x14 -> x0, blocking collectives: 397 us -> none  [move_rows(): whole = lax.all_gather(planes, 'gy', axis=2, tiled=True)]
    all_to_all x0 -> x8, blocking collectives: none -> 72.9 us  [move_rows(): lax.all_to_all(jnp.stack([planes] * lax.axis_size('gy')), 'gy', 0, 0)]
    all_to_all x0 -> x6, starting transfers between devices: none -> 37.2 us  [move_rows(): lax.all_to_all(jnp.stack([planes] * lax.axis_size('gy')), 'gy', 0, 0)]
    all_to_all x0 -> x6, waiting for transfers between devices: none -> 30.3 us  [move_rows(): lax.all_to_all(jnp.stack([planes] * lax.axis_size('gy')), 'gy', 0, 0)]
    ppermute x14, waiting for transfers between devices: 34.4 us -> 56.4 us  [extended(): after = lax.ppermute(first, axis, down)]
    ppermute x14, starting transfers between devices: 17.7 us -> 37 us  [extended(): before = lax.ppermute(last, axis, up)]
    ppermute x14, starting transfers between devices: 20.2 us -> 1.94 us  [extended(): after = lax.ppermute(first, axis, down)]
  transfers between devices with their start and end apart: 56 -> 62, of which waited for: 40 -> 45; matrix products, arithmetic and copies ran while one was open for 1% -> 1% of each run, Pallas kernels for 0% -> 0%
where the time goes in v1:
time: 368 us; the launch traced here: 367 us
  starting transfers between devices  152 us (41%)
  waiting for transfers between devices  120 us (33%)
  blocking collectives  72.9 us (20%)
  local copies, waits for them, and re-layouts  12.4 us (3%)
  other arithmetic  6.15 us (2%)
    ppermute x28, starting transfers between devices, from_behind(): return lax.ppermute(value, axis, pairs)  75.8 us
    all_to_all x8, blocking collectives, move_rows(): lax.all_to_all(jnp.stack([planes] * lax.axis_size('gy')), 'gy', 0, 0)  72.9 us
    ppermute x14, waiting for transfers between devices, extended(): after = lax.ppermute(first, axis, down)  56.4 us
    all_to_all x6, starting transfers between devices, move_rows(): lax.all_to_all(jnp.stack([planes] * lax.axis_size('gy')), 'gy', 0, 0)  37.2 us
    ppermute x14, starting transfers between devices, extended(): before = lax.ppermute(last, axis, up)  37 us
    all_to_all x6, waiting for transfers between devices, move_rows(): lax.all_to_all(jnp.stack([planes] * lax.axis_size('gy')), 'gy', 0, 0)  30.3 us
    ppermute x28, waiting for transfers between devices, from_behind(): return lax.ppermute(value, axis, pairs)  16.8 us
    ppermute x14, waiting for transfers between devices, extended(): before = lax.ppermute(last, axis, up)  16.5 us
  transfers between devices with their start and end apart: 62, of which 45 were waited for; matrix products, arithmetic and copies ran while one was open for 1% of the time, Pallas kernels for 0%

profile of v1, /device:TPU:14, one launch (start us, length us, event | category | flops | bytes accessed | tf_op | source)
XLA Modules:
  0.0 367.1 jit_solution(13462691082775376220)
XLA Ops:
  0.8 5.4 %collective-permute-start.1 = (f32[4,1,16,128]{3,2,1,0:T(8,128)S(1)}, f32[4,1,16,128]{3,2,1,0:T(8,128)S(1)}, u32[]{:S(2)}, u32[]{:S(2)}) collective-permute-start(f32[4,1,16,128]{3,2,1,0:T(8,128)S(1)} %get-tuple-element.40), channel_id=1, source_target_pairs={{0,120},{8,0},{16,8},{24,16},{32,24},{40,32},{48,40},{56,48},{64,5... | collective-permute-start | bytes 98312 | tf_op jit(solution)/shard_map/ppermute | solution.py:14
  9.6 5.8 %all-to-all-start = ((f32[8,4,2,16,128]{4,3,2,1,0:T(8,128)}), f32[8,4,2,16,128]{4,3,2,1,0:T(8,128)S(1)}, u32[]{:S(2)}, u32[]{:S(2)}) async-start(f32[8,4,2,16,128]{4,3,2,1,0:T(8,128)} %stack.48), calls=%async_computation | async-start | bytes 1048576 | tf_op jit(solution)/shard_map/all_to_all | solution.py:57
  15.8 6.5 %all-to-all-done = f32[8,4,2,16,128]{4,3,2,1,0:T(8,128)S(1)} async-done(((f32[8,4,2,16,128]{4,3,2,1,0:T(8,128)}), f32[8,4,2,16,128]{4,3,2,1,0:T(8,128)S(1)}, u32[]{:S(2)}, u32[]{:S(2)}) %all-to-all-start) | async-done | bytes 524320 | tf_op jit(solution)/shard_map/all_to_all | solution.py:57
  29.4 5.3 %collective-permute-start.5 = (f32[3,1,16,128]{3,2,1,0:T(8,128)S(1)}, f32[3,1,16,128]{3,2,1,0:T(8,128)S(1)}, u32[]{:S(2)}, u32[]{:S(2)}) collective-permute-start(f32[3,1,16,128]{3,2,1,0:T(8,128)S(1)} %get-tuple-element.33), channel_id=1, source_target_pairs={{0,120},{8,0},{16,8},{24,16},{32,24},{40,32},{48,40},{56,48},{64,5... | collective-permute-start | bytes 73736 | tf_op jit(solution)/shard_map/ppermute | solution.py:14
  37.0 7.5 %all-to-all-start.1 = ((f32[8,3,2,16,128]{4,3,2,1,0:T(8,128)}), f32[8,3,2,16,128]{4,3,2,1,0:T(8,128)S(1)}, u32[]{:S(2)}, u32[]{:S(2)}) async-start(f32[8,3,2,16,128]{4,3,2,1,0:T(8,128)} %stack.50), calls=%async_computation.1 | async-start | bytes 786432 | tf_op jit(solution)/shard_map/all_to_all | solution.py:57
  44.7 6.3 %all-to-all-done.1 = f32[8,3,2,16,128]{4,3,2,1,0:T(8,128)S(1)} async-done(((f32[8,3,2,16,128]{4,3,2,1,0:T(8,128)}), f32[8,3,2,16,128]{4,3,2,1,0:T(8,128)S(1)}, u32[]{:S(2)}, u32[]{:S(2)}) %all-to-all-start.1) | async-done | bytes 393248 | tf_op jit(solution)/shard_map/all_to_all | solution.py:57
  59.6 5.3 %collective-permute-start.9 = (f32[1,1,16,128]{3,2,1,0:T(8,128)S(1)}, f32[1,1,16,128]{3,2,1,0:T(8,128)S(1)}, u32[]{:S(2)}, u32[]{:S(2)}) collective-permute-start(f32[1,1,16,128]{3,2,1,0:T(8,128)S(1)} %get-tuple-element.138), channel_id=1, source_target_pairs={{0,120},{8,0},{16,8},{24,16},{32,24},{40,32},{48,40},{56,48},{64,5... | collective-permute-start | bytes 24584 | tf_op jit(solution)/shard_map/ppermute | solution.py:14
  66.4 9.1 %all_to_all.70 = f32[8,1,2,16,128]{4,3,2,1,0:T(8,128)S(1)} all-to-all(f32[8,1,2,16,128]{4,3,2,1,0:T(8,128)S(1)} %stack.51), channel_id=1, replica_groups=mesh['gx'=16,'gy'=8] {'gy'}, dimensions={0} | all-to-all | bytes 262144 | tf_op jit(solution)/shard_map/all_to_all | solution.py:57
  84.4 5.3 %collective-permute-start.13 = (f32[1,1,16,128]{3,2,1,0:T(8,128)S(1)}, f32[1,1,16,128]{3,2,1,0:T(8,128)S(1)}, u32[]{:S(2)}, u32[]{:S(2)}) collective-permute-start(f32[1,1,16,128]{3,2,1,0:T(8,128)S(1)} %get-tuple-element.136), channel_id=1, source_target_pairs={{0,120},{8,0},{16,8},{24,16},{32,24},{40,32},{48,40},{56,48},{64,5... | collective-permute-start | bytes 24584 | tf_op jit(solution)/shard_map/ppermute | solution.py:14
  91.1 9.1 %all_to_all.71 = f32[8,1,2,16,128]{4,3,2,1,0:T(8,128)S(1)} all-to-all(f32[8,1,2,16,128]{4,3,2,1,0:T(8,128)S(1)} %stack.52), channel_id=1, replica_groups=mesh['gx'=16,'gy'=8] {'gy'}, dimensions={0} | all-to-all | bytes 262144 | tf_op jit(solution)/shard_map/all_to_all | solution.py:57
  109.2 5.3 %collective-permute-start.17 = (f32[1,1,16,128]{3,2,1,0:T(8,128)S(1)}, f32[1,1,16,128]{3,2,1,0:T(8,128)S(1)}, u32[]{:S(2)}, u32[]{:S(2)}) collective-permute-start(f32[1,1,16,128]{3,2,1,0:T(8,128)S(1)} %get-tuple-element.134), channel_id=1, source_target_pairs={{0,120},{8,0},{16,8},{24,16},{32,24},{40,32},{48,40},{56,48},{64,5... | collective-permute-start | bytes 24584 | tf_op jit(solution)/shard_map/ppermute | solution.py:14
  115.9 9.1 %all_to_all.72 = f32[8,1,2,16,128]{4,3,2,1,0:T(8,128)S(1)} all-to-all(f32[8,1,2,16,128]{4,3,2,1,0:T(8,128)S(1)} %stack.53), channel_id=1, replica_groups=mesh['gx'=16,'gy'=8] {'gy'}, dimensions={0} | all-to-all | bytes 262144 | tf_op jit(solution)/shard_map/all_to_all | solution.py:57
  133.9 5.3 %collective-permute-start.21 = (f32[1,1,16,128]{3,2,1,0:T(8,128)S(1)}, f32[1,1,16,128]{3,2,1,0:T(8,128)S(1)}, u32[]{:S(2)}, u32[]{:S(2)}) collective-permute-start(f32[1,1,16,128]{3,2,1,0:T(8,128)S(1)} %get-tuple-element.132), channel_id=1, source_target_pairs={{0,120},{8,0},{16,8},{24,16},{32,24},{40,32},{48,40},{56,48},{64,5... | collective-permute-start | bytes 24584 | tf_op jit(solution)/shard_map/ppermute | solution.py:14
  140.7 9.1 %all_to_all.73 = f32[8,1,2,16,128]{4,3,2,1,0:T(8,128)S(1)} all-to-all(f32[8,1,2,16,128]{4,3,2,1,0:T(8,128)S(1)} %stack.54), channel_id=1, replica_groups=mesh['gx'=16,'gy'=8] {'gy'}, dimensions={0} | all-to-all | bytes 262144 | tf_op jit(solution)/shard_map/all_to_all | solution.py:57
  158.7 5.3 %collective-permute-start.25 = (f32[1,1,16,128]{3,2,1,0:T(8,128)S(1)}, f32[1,1,16,128]{3,2,1,0:T(8,128)S(1)}, u32[]{:S(2)}, u32[]{:S(2)}) collective-permute-start(f32[1,1,16,128]{3,2,1,0:T(8,128)S(1)} %get-tuple-element.130), channel_id=1, source_target_pairs={{0,120},{8,0},{16,8},{24,16},{32,24},{40,32},{48,40},{56,48},{64,5... | collective-permute-start | bytes 24584 | tf_op jit(solution)/shard_map/ppermute | solution.py:14
  166.1 5.4 %all-to-all-start.6 = ((f32[8,1,2,16,128]{4,3,2,1,0:T(8,128)}), f32[8,1,2,16,128]{4,3,2,1,0:T(8,128)S(1)}, u32[]{:S(2)}, u32[]{:S(2)}) async-start(f32[8,1,2,16,128]{4,3,2,1,0:T(8,128)} %stack.55), calls=%async_computation.6 | async-start | bytes 262144 | tf_op jit(solution)/shard_map/all_to_all | solution.py:57
  184.8 5.3 %collective-permute-start.29 = (f32[4,1,16,128]{3,2,1,0:T(8,128)S(1)}, f32[4,1,16,128]{3,2,1,0:T(8,128)S(1)}, u32[]{:S(2)}, u32[]{:S(2)}) collective-permute-start(f32[4,1,16,128]{3,2,1,0:T(8,128)S(1)} %get-tuple-element.26), channel_id=1, source_target_pairs={{0,120},{8,0},{16,8},{24,16},{32,24},{40,32},{48,40},{56,48},{64,5... | collective-permute-start | bytes 98312 | tf_op jit(solution)/shard_map/ppermute | solution.py:14
  193.2 5.4 %all-to-all-start.7 = ((f32[8,4,2,16,128]{4,3,2,1,0:T(8,128)}), f32[8,4,2,16,128]{4,3,2,1,0:T(8,128)S(1)}, u32[]{:S(2)}, u32[]{:S(2)}) async-start(f32[8,4,2,16,128]{4,3,2,1,0:T(8,128)} %stack.59), calls=%async_computation.7 | async-start | bytes 1048576 | tf_op jit(solution)/shard_map/all_to_all | solution.py:57
  199.8 4.8 %all-to-all-done.7 = f32[8,4,2,16,128]{4,3,2,1,0:T(8,128)S(1)} async-done(((f32[8,4,2,16,128]{4,3,2,1,0:T(8,128)}), f32[8,4,2,16,128]{4,3,2,1,0:T(8,128)S(1)}, u32[]{:S(2)}, u32[]{:S(2)}) %all-to-all-start.7) | async-done | bytes 524320 | tf_op jit(solution)/shard_map/all_to_all | solution.py:57
  212.4 5.3 %collective-permute-start.33 = (f32[3,1,16,128]{3,2,1,0:T(8,128)S(1)}, f32[3,1,16,128]{3,2,1,0:T(8,128)S(1)}, u32[]{:S(2)}, u32[]{:S(2)}) collective-permute-start(f32[3,1,16,128]{3,2,1,0:T(8,128)S(1)} %get-tuple-element.24), channel_id=1, source_target_pairs={{0,120},{8,0},{16,8},{24,16},{32,24},{40,32},{48,40},{56,48},{64,5... | collective-permute-start | bytes 73736 | tf_op jit(solution)/shard_map/ppermute | solution.py:14
  220.1 7.6 %all-to-all-start.8 = ((f32[8,3,2,16,128]{4,3,2,1,0:T(8,128)}), f32[8,3,2,16,128]{4,3,2,1,0:T(8,128)S(1)}, u32[]{:S(2)}, u32[]{:S(2)}) async-start(f32[8,3,2,16,128]{4,3,2,1,0:T(8,128)} %stack.63), calls=%async_computation.8 | async-start | bytes 786432 | tf_op jit(solution)/shard_map/all_to_all | solution.py:57
  227.8 5.1 %all-to-all-done.8 = f32[8,3,2,16,128]{4,3,2,1,0:T(8,128)S(1)} async-done(((f32[8,3,2,16,128]{4,3,2,1,0:T(8,128)}), f32[8,3,2,16,128]{4,3,2,1,0:T(8,128)S(1)}, u32[]{:S(2)}, u32[]{:S(2)}) %all-to-all-start.8) | async-done | bytes 393248 | tf_op jit(solution)/shard_map/all_to_all | solution.py:57
  241.7 5.3 %collective-permute-start.37 = (f32[1,1,16,128]{3,2,1,0:T(8,128)S(1)}, f32[1,1,16,128]{3,2,1,0:T(8,128)S(1)}, u32[]{:S(2)}, u32[]{:S(2)}) collective-permute-start(f32[1,1,16,128]{3,2,1,0:T(8,128)S(1)} %get-tuple-element.118), channel_id=1, source_target_pairs={{0,120},{8,0},{16,8},{24,16},{32,24},{40,32},{48,40},{56,48},{64,5... | collective-permute-start | bytes 24584 | tf_op jit(solution)/shard_map/ppermute | solution.py:14
  248.5 9.1 %all_to_all.74 = f32[8,1,2,16,128]{4,3,2,1,0:T(8,128)S(1)} all-to-all(f32[8,1,2,16,128]{4,3,2,1,0:T(8,128)S(1)} %stack.64), channel_id=1, replica_groups=mesh['gx'=16,'gy'=8] {'gy'}, dimensions={0} | all-to-all | bytes 262144 | tf_op jit(solution)/shard_map/all_to_all | solution.py:57
  266.5 5.3 %collective-permute-start.41 = (f32[1,1,16,128]{3,2,1,0:T(8,128)S(1)}, f32[1,1,16,128]{3,2,1,0:T(8,128)S(1)}, u32[]{:S(2)}, u32[]{:S(2)}) collective-permute-start(f32[1,1,16,128]{3,2,1,0:T(8,128)S(1)} %get-tuple-element.116), channel_id=1, source_target_pairs={{0,120},{8,0},{16,8},{24,16},{32,24},{40,32},{48,40},{56,48},{64,5... | collective-permute-start | bytes 24584 | tf_op jit(solution)/shard_map/ppermute | solution.py:14
  273.3 9.1 %all_to_all.75 = f32[8,1,2,16,128]{4,3,2,1,0:T(8,128)S(1)} all-to-all(f32[8,1,2,16,128]{4,3,2,1,0:T(8,128)S(1)} %stack.65), channel_id=1, replica_groups=mesh['gx'=16,'gy'=8] {'gy'}, dimensions={0} | all-to-all | bytes 262144 | tf_op jit(solution)/shard_map/all_to_all | solution.py:57
  291.5 5.3 %collective-permute-start.45 = (f32[1,1,16,128]{3,2,1,0:T(8,128)S(1)}, f32[1,1,16,128]{3,2,1,0:T(8,128)S(1)}, u32[]{:S(2)}, u32[]{:S(2)}) collective-permute-start(f32[1,1,16,128]{3,2,1,0:T(8,128)S(1)} %get-tuple-element.114), channel_id=1, source_target_pairs={{0,120},{8,0},{16,8},{24,16},{32,24},{40,32},{48,40},{56,48},{64,5... | collective-permute-start | bytes 24584 | tf_op jit(solution)/shard_map/ppermute | solution.py:14
  298.2 9.1 %all_to_all.76 = f32[8,1,2,16,128]{4,3,2,1,0:T(8,128)S(1)} all-to-all(f32[8,1,2,16,128]{4,3,2,1,0:T(8,128)S(1)} %stack.66), channel_id=1, replica_groups=mesh['gx'=16,'gy'=8] {'gy'}, dimensions={0} | all-to-all | bytes 262144 | tf_op jit(solution)/shard_map/all_to_all | solution.py:57
  316.3 5.3 %collective-permute-start.49 = (f32[1,1,16,128]{3,2,1,0:T(8,128)S(1)}, f32[1,1,16,128]{3,2,1,0:T(8,128)S(1)}, u32[]{:S(2)}, u32[]{:S(2)}) collective-permute-start(f32[1,1,16,128]{3,2,1,0:T(8,128)S(1)} %get-tuple-element.112), channel_id=1, source_target_pairs={{0,120},{8,0},{16,8},{24,16},{32,24},{40,32},{48,40},{56,48},{64,5... | collective-permute-start | bytes 24584 | tf_op jit(solution)/shard_map/ppermute | solution.py:14
  323.0 9.1 %all_to_all.77 = f32[8,1,2,16,128]{4,3,2,1,0:T(8,128)S(1)} all-to-all(f32[8,1,2,16,128]{4,3,2,1,0:T(8,128)S(1)} %stack.67), channel_id=1, replica_groups=mesh['gx'=16,'gy'=8] {'gy'}, dimensions={0} | all-to-all | bytes 262144 | tf_op jit(solution)/shard_map/all_to_all | solution.py:57
  341.1 5.3 %collective-permute-start.53 = (f32[1,1,16,128]{3,2,1,0:T(8,128)S(1)}, f32[1,1,16,128]{3,2,1,0:T(8,128)S(1)}, u32[]{:S(2)}, u32[]{:S(2)}) collective-permute-start(f32[1,1,16,128]{3,2,1,0:T(8,128)S(1)} %get-tuple-element.106), channel_id=1, source_target_pairs={{0,120},{8,0},{16,8},{24,16},{32,24},{40,32},{48,40},{56,48},{64,5... | collective-permute-start | bytes 24584 | tf_op jit(solution)/shard_map/ppermute | solution.py:14
  348.4 5.4 %all-to-all-start.13 = ((f32[8,1,2,16,128]{4,3,2,1,0:T(8,128)}), f32[8,1,2,16,128]{4,3,2,1,0:T(8,128)S(1)}, u32[]{:S(2)}, u32[]{:S(2)}) async-start(f32[8,1,2,16,128]{4,3,2,1,0:T(8,128)} %stack.68), calls=%async_computation.13 | async-start | bytes 262144 | tf_op jit(solution)/shard_map/all_to_all | solution.py:57
  (281 shorter events, 155.8 us)
Async XLA Ops:
  0.8 8.0 %collective-permute-start = (f32[4,1,16,128]{3,2,1,0:T(8,128)S(1)}, f32[4,1,16,128]{3,2,1,0:T(8,128)S(1)}, u32[]{:S(2)}, u32[]{:S(2)}) collective-permute-start(f32[4,1,16,128]{3,2,1,0:T(8,128)S(1)} %get-tuple-element.39), channel_id=1, source_target_pairs={{0,8},{8,16},{16,24},{24,32},{32,40},{40,48},{48,56},{56,64},{64,7... | collective-permute-start | bytes 98312 | tf_op jit(solution)/shard_map/ppermute | solution.py:14
  0.8 8.0 %collective-permute-start.1 = (f32[4,1,16,128]{3,2,1,0:T(8,128)S(1)}, f32[4,1,16,128]{3,2,1,0:T(8,128)S(1)}, u32[]{:S(2)}, u32[]{:S(2)}) collective-permute-start(f32[4,1,16,128]{3,2,1,0:T(8,128)S(1)} %get-tuple-element.40), channel_id=1, source_target_pairs={{0,120},{8,0},{16,8},{24,16},{32,24},{40,32},{48,40},{56,48},{64,5... | collective-permute-start | bytes 98312 | tf_op jit(solution)/shard_map/ppermute | solution.py:14
  9.6 12.7 %all-to-all-start = ((f32[8,4,2,16,128]{4,3,2,1,0:T(8,128)}), f32[8,4,2,16,128]{4,3,2,1,0:T(8,128)S(1)}, u32[]{:S(2)}, u32[]{:S(2)}) async-start(f32[8,4,2,16,128]{4,3,2,1,0:T(8,128)} %stack.48), calls=%async_computation | async-start | bytes 1048576 | tf_op jit(solution)/shard_map/all_to_all | solution.py:57
  29.3 6.9 %collective-permute-start.4 = (f32[3,1,16,128]{3,2,1,0:T(8,128)S(1)}, f32[3,1,16,128]{3,2,1,0:T(8,128)S(1)}, u32[]{:S(2)}, u32[]{:S(2)}) collective-permute-start(f32[3,1,16,128]{3,2,1,0:T(8,128)S(1)} %get-tuple-element.32), channel_id=1, source_target_pairs={{0,8},{8,16},{16,24},{24,32},{32,40},{40,48},{48,56},{56,64},{64,7... | collective-permute-start | bytes 73736 | tf_op jit(solution)/shard_map/ppermute | solution.py:14
  29.4 6.9 %collective-permute-start.5 = (f32[3,1,16,128]{3,2,1,0:T(8,128)S(1)}, f32[3,1,16,128]{3,2,1,0:T(8,128)S(1)}, u32[]{:S(2)}, u32[]{:S(2)}) collective-permute-start(f32[3,1,16,128]{3,2,1,0:T(8,128)S(1)} %get-tuple-element.33), channel_id=1, source_target_pairs={{0,120},{8,0},{16,8},{24,16},{32,24},{40,32},{48,40},{56,48},{64,5... | collective-permute-start | bytes 73736 | tf_op jit(solution)/shard_map/ppermute | solution.py:14
  37.0 13.9 %all-to-all-start.1 = ((f32[8,3,2,16,128]{4,3,2,1,0:T(8,128)}), f32[8,3,2,16,128]{4,3,2,1,0:T(8,128)S(1)}, u32[]{:S(2)}, u32[]{:S(2)}) async-start(f32[8,3,2,16,128]{4,3,2,1,0:T(8,128)} %stack.50), calls=%async_computation.1 | async-start | bytes 786432 | tf_op jit(solution)/shard_map/all_to_all | solution.py:57
  59.6 6.8 %collective-permute-start.8 = (f32[1,1,16,128]{3,2,1,0:T(8,128)S(1)}, f32[1,1,16,128]{3,2,1,0:T(8,128)S(1)}, u32[]{:S(2)}, u32[]{:S(2)}) collective-permute-start(f32[1,1,16,128]{3,2,1,0:T(8,128)S(1)} %get-tuple-element.137), channel_id=1, source_target_pairs={{0,8},{8,16},{16,24},{24,32},{32,40},{40,48},{48,56},{56,64},{64,7... | collective-permute-start | bytes 24584 | tf_op jit(solution)/shard_map/ppermute | solution.py:14
  59.6 6.7 %collective-permute-start.9 = (f32[1,1,16,128]{3,2,1,0:T(8,128)S(1)}, f32[1,1,16,128]{3,2,1,0:T(8,128)S(1)}, u32[]{:S(2)}, u32[]{:S(2)}) collective-permute-start(f32[1,1,16,128]{3,2,1,0:T(8,128)S(1)} %get-tuple-element.138), channel_id=1, source_target_pairs={{0,120},{8,0},{16,8},{24,16},{32,24},{40,32},{48,40},{56,48},{64,5... | collective-permute-start | bytes 24584 | tf_op jit(solution)/shard_map/ppermute | solution.py:14
  84.3 6.8 %collective-permute-start.12 = (f32[1,1,16,128]{3,2,1,0:T(8,128)S(1)}, f32[1,1,16,128]{3,2,1,0:T(8,128)S(1)}, u32[]{:S(2)}, u32[]{:S(2)}) collective-permute-start(f32[1,1,16,128]{3,2,1,0:T(8,128)S(1)} %get-tuple-element.135), channel_id=1, source_target_pairs={{0,8},{8,16},{16,24},{24,32},{32,40},{40,48},{48,56},{56,64},{64,7... | collective-permute-start | bytes 24584 | tf_op jit(solution)/shard_map/ppermute | solution.py:14
  84.4 6.7 %collective-permute-start.13 = (f32[1,1,16,128]{3,2,1,0:T(8,128)S(1)}, f32[1,1,16,128]{3,2,1,0:T(8,128)S(1)}, u32[]{:S(2)}, u32[]{:S(2)}) collective-permute-start(f32[1,1,16,128]{3,2,1,0:T(8,128)S(1)} %get-tuple-element.136), channel_id=1, source_target_pairs={{0,120},{8,0},{16,8},{24,16},{32,24},{40,32},{48,40},{56,48},{64,5... | collective-permute-start | bytes 24584 | tf_op jit(solution)/shard_map/ppermute | solution.py:14
  109.1 6.8 %collective-permute-start.16 = (f32[1,1,16,128]{3,2,1,0:T(8,128)S(1)}, f32[1,1,16,128]{3,2,1,0:T(8,128)S(1)}, u32[]{:S(2)}, u32[]{:S(2)}) collective-permute-start(f32[1,1,16,128]{3,2,1,0:T(8,128)S(1)} %get-tuple-element.133), channel_id=1, source_target_pairs={{0,8},{8,16},{16,24},{24,32},{32,40},{40,48},{48,56},{56,64},{64,7... | collective-permute-start | bytes 24584 | tf_op jit(solution)/shard_map/ppermute | solution.py:14
  109.2 6.7 %collective-permute-start.17 = (f32[1,1,16,128]{3,2,1,0:T(8,128)S(1)}, f32[1,1,16,128]{3,2,1,0:T(8,128)S(1)}, u32[]{:S(2)}, u32[]{:S(2)}) collective-permute-start(f32[1,1,16,128]{3,2,1,0:T(8,128)S(1)} %get-tuple-element.134), channel_id=1, source_target_pairs={{0,120},{8,0},{16,8},{24,16},{32,24},{40,32},{48,40},{56,48},{64,5... | collective-permute-start | bytes 24584 | tf_op jit(solution)/shard_map/ppermute | solution.py:14
  133.9 6.8 %collective-permute-start.20 = (f32[1,1,16,128]{3,2,1,0:T(8,128)S(1)}, f32[1,1,16,128]{3,2,1,0:T(8,128)S(1)}, u32[]{:S(2)}, u32[]{:S(2)}) collective-permute-start(f32[1,1,16,128]{3,2,1,0:T(8,128)S(1)} %get-tuple-element.131), channel_id=1, source_target_pairs={{0,8},{8,16},{16,24},{24,32},{32,40},{40,48},{48,56},{56,64},{64,7... | collective-permute-start | bytes 24584 | tf_op jit(solution)/shard_map/ppermute | solution.py:14
  133.9 6.7 %collective-permute-start.21 = (f32[1,1,16,128]{3,2,1,0:T(8,128)S(1)}, f32[1,1,16,128]{3,2,1,0:T(8,128)S(1)}, u32[]{:S(2)}, u32[]{:S(2)}) collective-permute-start(f32[1,1,16,128]{3,2,1,0:T(8,128)S(1)} %get-tuple-element.132), channel_id=1, source_target_pairs={{0,120},{8,0},{16,8},{24,16},{32,24},{40,32},{48,40},{56,48},{64,5... | collective-permute-start | bytes 24584 | tf_op jit(solution)/shard_map/ppermute | solution.py:14
  158.6 6.8 %collective-permute-start.24 = (f32[1,1,16,128]{3,2,1,0:T(8,128)S(1)}, f32[1,1,16,128]{3,2,1,0:T(8,128)S(1)}, u32[]{:S(2)}, u32[]{:S(2)}) collective-permute-start(f32[1,1,16,128]{3,2,1,0:T(8,128)S(1)} %get-tuple-element.129), channel_id=1, source_target_pairs={{0,8},{8,16},{16,24},{24,32},{32,40},{40,48},{48,56},{56,64},{64,7... | collective-permute-start | bytes 24584 | tf_op jit(solution)/shard_map/ppermute | solution.py:14
  158.7 6.7 %collective-permute-start.25 = (f32[1,1,16,128]{3,2,1,0:T(8,128)S(1)}, f32[1,1,16,128]{3,2,1,0:T(8,128)S(1)}, u32[]{:S(2)}, u32[]{:S(2)}) collective-permute-start(f32[1,1,16,128]{3,2,1,0:T(8,128)S(1)} %get-tuple-element.130), channel_id=1, source_target_pairs={{0,120},{8,0},{16,8},{24,16},{32,24},{40,32},{48,40},{56,48},{64,5... | collective-permute-start | bytes 24584 | tf_op jit(solution)/shard_map/ppermute | solution.py:14
  166.1 9.3 %all-to-all-start.6 = ((f32[8,1,2,16,128]{4,3,2,1,0:T(8,128)}), f32[8,1,2,16,128]{4,3,2,1,0:T(8,128)S(1)}, u32[]{:S(2)}, u32[]{:S(2)}) async-start(f32[8,1,2,16,128]{4,3,2,1,0:T(8,128)} %stack.55), calls=%async_computation.6 | async-start | bytes 262144 | tf_op jit(solution)/shard_map/all_to_all | solution.py:57
  184.7 7.0 %collective-permute-start.28 = (f32[4,1,16,128]{3,2,1,0:T(8,128)S(1)}, f32[4,1,16,128]{3,2,1,0:T(8,128)S(1)}, u32[]{:S(2)}, u32[]{:S(2)}) collective-permute-start(f32[4,1,16,128]{3,2,1,0:T(8,128)S(1)} %get-tuple-element.25), channel_id=1, source_target_pairs={{0,8},{8,16},{16,24},{24,32},{32,40},{40,48},{48,56},{56,64},{64,7... | collective-permute-start | bytes 98312 | tf_op jit(solution)/shard_map/ppermute | solution.py:14
  184.8 6.9 %collective-permute-start.29 = (f32[4,1,16,128]{3,2,1,0:T(8,128)S(1)}, f32[4,1,16,128]{3,2,1,0:T(8,128)S(1)}, u32[]{:S(2)}, u32[]{:S(2)}) collective-permute-start(f32[4,1,16,128]{3,2,1,0:T(8,128)S(1)} %get-tuple-element.26), channel_id=1, source_target_pairs={{0,120},{8,0},{16,8},{24,16},{32,24},{40,32},{48,40},{56,48},{64,5... | collective-permute-start | bytes 98312 | tf_op jit(solution)/shard_map/ppermute | solution.py:14
  193.2 11.4 %all-to-all-start.7 = ((f32[8,4,2,16,128]{4,3,2,1,0:T(8,128)}), f32[8,4,2,16,128]{4,3,2,1,0:T(8,128)S(1)}, u32[]{:S(2)}, u32[]{:S(2)}) async-start(f32[8,4,2,16,128]{4,3,2,1,0:T(8,128)} %stack.59), calls=%async_computation.7 | async-start | bytes 1048576 | tf_op jit(solution)/shard_map/all_to_all | solution.py:57
  212.3 6.9 %collective-permute-start.32 = (f32[3,1,16,128]{3,2,1,0:T(8,128)S(1)}, f32[3,1,16,128]{3,2,1,0:T(8,128)S(1)}, u32[]{:S(2)}, u32[]{:S(2)}) collective-permute-start(f32[3,1,16,128]{3,2,1,0:T(8,128)S(1)} %get-tuple-element.23), channel_id=1, source_target_pairs={{0,8},{8,16},{16,24},{24,32},{32,40},{40,48},{48,56},{56,64},{64,7... | collective-permute-start | bytes 73736 | tf_op jit(solution)/shard_map/ppermute | solution.py:14
  212.4 6.9 %collective-permute-start.33 = (f32[3,1,16,128]{3,2,1,0:T(8,128)S(1)}, f32[3,1,16,128]{3,2,1,0:T(8,128)S(1)}, u32[]{:S(2)}, u32[]{:S(2)}) collective-permute-start(f32[3,1,16,128]{3,2,1,0:T(8,128)S(1)} %get-tuple-element.24), channel_id=1, source_target_pairs={{0,120},{8,0},{16,8},{24,16},{32,24},{40,32},{48,40},{56,48},{64,5... | collective-permute-start | bytes 73736 | tf_op jit(solution)/shard_map/ppermute | solution.py:14
  220.1 12.9 %all-to-all-start.8 = ((f32[8,3,2,16,128]{4,3,2,1,0:T(8,128)}), f32[8,3,2,16,128]{4,3,2,1,0:T(8,128)S(1)}, u32[]{:S(2)}, u32[]{:S(2)}) async-start(f32[8,3,2,16,128]{4,3,2,1,0:T(8,128)} %stack.63), calls=%async_computation.8 | async-start | bytes 786432 | tf_op jit(solution)/shard_map/all_to_all | solution.py:57
  241.7 6.8 %collective-permute-start.36 = (f32[1,1,16,128]{3,2,1,0:T(8,128)S(1)}, f32[1,1,16,128]{3,2,1,0:T(8,128)S(1)}, u32[]{:S(2)}, u32[]{:S(2)}) collective-permute-start(f32[1,1,16,128]{3,2,1,0:T(8,128)S(1)} %get-tuple-element.117), channel_id=1, source_target_pairs={{0,8},{8,16},{16,24},{24,32},{32,40},{40,48},{48,56},{56,64},{64,7... | collective-permute-start | bytes 24584 | tf_op jit(solution)/shard_map/ppermute | solution.py:14
  241.7 6.7 %collective-permute-start.37 = (f32[1,1,16,128]{3,2,1,0:T(8,128)S(1)}, f32[1,1,16,128]{3,2,1,0:T(8,128)S(1)}, u32[]{:S(2)}, u32[]{:S(2)}) collective-permute-start(f32[1,1,16,128]{3,2,1,0:T(8,128)S(1)} %get-tuple-element.118), channel_id=1, source_target_pairs={{0,120},{8,0},{16,8},{24,16},{32,24},{40,32},{48,40},{56,48},{64,5... | collective-permute-start | bytes 24584 | tf_op jit(solution)/shard_map/ppermute | solution.py:14
  266.4 6.8 %collective-permute-start.40 = (f32[1,1,16,128]{3,2,1,0:T(8,128)S(1)}, f32[1,1,16,128]{3,2,1,0:T(8,128)S(1)}, u32[]{:S(2)}, u32[]{:S(2)}) collective-permute-start(f32[1,1,16,128]{3,2,1,0:T(8,128)S(1)} %get-tuple-element.115), channel_id=1, source_target_pairs={{0,8},{8,16},{16,24},{24,32},{32,40},{40,48},{48,56},{56,64},{64,7... | collective-permute-start | bytes 24584 | tf_op jit(solution)/shard_map/ppermute | solution.py:14
  266.5 6.7 %collective-permute-start.41 = (f32[1,1,16,128]{3,2,1,0:T(8,128)S(1)}, f32[1,1,16,128]{3,2,1,0:T(8,128)S(1)}, u32[]{:S(2)}, u32[]{:S(2)}) collective-permute-start(f32[1,1,16,128]{3,2,1,0:T(8,128)S(1)} %get-tuple-element.116), channel_id=1, source_target_pairs={{0,120},{8,0},{16,8},{24,16},{32,24},{40,32},{48,40},{56,48},{64,5... | collective-permute-start | bytes 24584 | tf_op jit(solution)/shard_map/ppermute | solution.py:14
  291.4 6.8 %collective-permute-start.44 = (f32[1,1,16,128]{3,2,1,0:T(8,128)S(1)}, f32[1,1,16,128]{3,2,1,0:T(8,128)S(1)}, u32[]{:S(2)}, u32[]{:S(2)}) collective-permute-start(f32[1,1,16,128]{3,2,1,0:T(8,128)S(1)} %get-tuple-element.113), channel_id=1, source_target_pairs={{0,8},{8,16},{16,24},{24,32},{32,40},{40,48},{48,56},{56,64},{64,7... | collective-permute-start | bytes 24584 | tf_op jit(solution)/shard_map/ppermute | solution.py:14
  316.2 6.8 %collective-permute-start.48 = (f32[1,1,16,128]{3,2,1,0:T(8,128)S(1)}, f32[1,1,16,128]{3,2,1,0:T(8,128)S(1)}, u32[]{:S(2)}, u32[]{:S(2)}) collective-permute-start(f32[1,1,16,128]{3,2,1,0:T(8,128)S(1)} %get-tuple-element.111), channel_id=1, source_target_pairs={{0,8},{8,16},{16,24},{24,32},{32,40},{40,48},{48,56},{56,64},{64,7... | collective-permute-start | bytes 24584 | tf_op jit(solution)/shard_map/ppermute | solution.py:14
  316.3 6.7 %collective-permute-start.49 = (f32[1,1,16,128]{3,2,1,0:T(8,128)S(1)}, f32[1,1,16,128]{3,2,1,0:T(8,128)S(1)}, u32[]{:S(2)}, u32[]{:S(2)}) collective-permute-start(f32[1,1,16,128]{3,2,1,0:T(8,128)S(1)} %get-tuple-element.112), channel_id=1, source_target_pairs={{0,120},{8,0},{16,8},{24,16},{32,24},{40,32},{48,40},{56,48},{64,5... | collective-permute-start | bytes 24584 | tf_op jit(solution)/shard_map/ppermute | solution.py:14
  341.0 6.8 %collective-permute-start.52 = (f32[1,1,16,128]{3,2,1,0:T(8,128)S(1)}, f32[1,1,16,128]{3,2,1,0:T(8,128)S(1)}, u32[]{:S(2)}, u32[]{:S(2)}) collective-permute-start(f32[1,1,16,128]{3,2,1,0:T(8,128)S(1)} %get-tuple-element.105), channel_id=1, source_target_pairs={{0,8},{8,16},{16,24},{24,32},{32,40},{40,48},{48,56},{56,64},{64,7... | collective-permute-start | bytes 24584 | tf_op jit(solution)/shard_map/ppermute | solution.py:14
  348.4 9.3 %all-to-all-start.13 = ((f32[8,1,2,16,128]{4,3,2,1,0:T(8,128)}), f32[8,1,2,16,128]{4,3,2,1,0:T(8,128)S(1)}, u32[]{:S(2)}, u32[]{:S(2)}) async-start(f32[8,1,2,16,128]{4,3,2,1,0:T(8,128)} %stack.68), calls=%async_computation.13 | async-start | bytes 262144 | tf_op jit(solution)/shard_map/all_to_all | solution.py:57
  (38 other events, 173.6 us)
